TPU v7x, 32 devices: a whole 2x2x4 slice. The times are simulated.
32 devices in a mesh: section: 2 (over y), expert: 16 (over z, x, core).
Axes of the slice: x: 2, y: 2, z: 4, core: 2. Of those that a mesh axis runs over, the one named last changes fastest.
Arguments:
- in_flight: bfloat16 [2, 1024, 2048], P('section', 'expert'), may hold values from -6 to 6
- entering: bfloat16 [1, 1024, 2048], P(None, 'expert'), may hold values from -6 to 6
- norm_gain: bfloat16 [2, 2048], P('section'), may hold values from 0.5 to 1.5
- w_gate: bfloat16 [2, 16, 2048, 768], P('section', 'expert'), may hold values from -0.125 to 0.125
- w_up: bfloat16 [2, 16, 2048, 768], P('section', 'expert'), may hold values from -0.125 to 0.125
- w_down: bfloat16 [2, 16, 768, 2048], P('section', 'expert'), may hold values from -0.21875 to 0.21875
- routes: int32 [2, 2, 1024, 8], P('section', None, 'expert'), may hold values from 0 to 15, all different within a row; in each aligned block of 32 rows (0 to 31, 32 to 63, ..., all dimensions but the last counted through in order) at most 24 rows name the same one
- combine_weight: float32 [2, 2, 1024, 8], P('section', None, 'expert'), may hold values from 0.2 to 0.6
Outputs:
- trace: bfloat16 [2, 2, 1024, 2048], P(None, 'section', 'expert')
Inputs may be any that keep to these rules, and one draw needn't show every extreme that they name: `routes`: each row names 8 different experts. In each aligned block of 32 rows (all leading dimensions taken together, in order) no expert is named by more than 24 rows, a bound that some block reaches.
All inputs are finite; a program needn't handle non-finite values.
Results may differ from a plain program's by a relative error of at most 0.0085.
Values may be sent and summed in bfloat16 or wider, within the bound.
A program may use at most 128 MiB of HBM per device.

v0:
```python
import jax
import jax.numpy as jnp
from jax import lax
from jax.sharding import PartitionSpec as P

TICKS = 2


EPSILON = 1e-06


def passed_along(x, axis, by):
    devices = lax.axis_size(axis)
    pairs = [(i, i + by) for i in range(devices) if 0 <= i + by < devices]
    return lax.ppermute(x, axis, pairs)


def rms_normed(hidden_rows, norm_gain):
    as_float = hidden_rows.astype(jnp.float32)
    inv_scale = lax.rsqrt(jnp.mean(as_float * as_float, axis=-1, keepdims=True) + EPSILON)
    return (as_float * inv_scale * norm_gain.astype(jnp.float32)).astype(jnp.bfloat16)


def slot_table(route_ids, experts, capacity):
    group_count, row_count, top_count = route_ids.shape
    expert_marks = (route_ids[..., None] == jnp.arange(experts, dtype=jnp.int32)).astype(jnp.int32)
    expert_marks = expert_marks.reshape(group_count, row_count * top_count, experts)
    earlier_marks = jnp.cumsum(expert_marks, axis=1) - expert_marks
    slot_index = jnp.sum(earlier_marks * expert_marks, axis=-1).reshape(
        group_count, row_count, top_count
    )
    group_index = jnp.arange(group_count, dtype=jnp.int32)[:, None, None]
    group_width = group_count * capacity
    positions = route_ids * group_width + group_index * capacity + slot_index
    return positions.reshape(group_count * row_count, top_count)


def mix_block(
    hidden_rows, normed_rows, route_ids, combine, gate_w, up_w, down_w, experts, capacity
):
    group_count = route_ids.shape[0]
    row_count = hidden_rows.shape[0]
    top_count = route_ids.shape[-1]
    model_width = hidden_rows.shape[1]
    positions = slot_table(route_ids, experts, capacity)
    slot_total = experts * group_count * capacity
    flat_slots = positions.reshape(-1)
    pick_table = flat_slots[None, :] == jnp.arange(slot_total, dtype=jnp.int32)[:, None]
    pick_table = jnp.sum(
        pick_table.reshape(slot_total, row_count, top_count).astype(jnp.int32), axis=-1
    ).astype(jnp.bfloat16)
    outgoing = jnp.dot(pick_table, normed_rows, preferred_element_type=jnp.float32).astype(
        jnp.bfloat16
    )
    outgoing = outgoing.reshape(experts, group_count * capacity, model_width)
    received = lax.all_to_all(outgoing, "expert", split_axis=0, concat_axis=0, tiled=True)
    row_shape = received.shape
    inputs = received.reshape(-1, row_shape[-1])
    gate_sum = jnp.dot(inputs, gate_w, preferred_element_type=jnp.float32)
    up_sum = jnp.dot(inputs, up_w, preferred_element_type=jnp.float32)
    hidden = (jax.nn.silu(gate_sum) * up_sum).astype(jnp.bfloat16)
    result = jnp.dot(hidden, down_w, preferred_element_type=jnp.float32).astype(jnp.bfloat16)
    returned = lax.all_to_all(
        result.reshape(row_shape), "expert", split_axis=0, concat_axis=0, tiled=True
    )
    returned = returned.reshape(slot_total, model_width)
    residual = hidden_rows.astype(jnp.float32)
    hit_table = (flat_slots[:, None] == jnp.arange(slot_total, dtype=jnp.int32)[None, :]).astype(
        jnp.float32
    )
    mixing = jnp.sum(
        hit_table.reshape(row_count, top_count, slot_total) * combine[:, :, None], axis=1
    )
    mixing_high = mixing.astype(jnp.bfloat16)
    mixing_low = (mixing - mixing_high.astype(jnp.float32)).astype(jnp.bfloat16)
    branch_sum = jnp.dot(mixing_high, returned, preferred_element_type=jnp.float32)
    branch_sum = branch_sum + jnp.dot(mixing_low, returned, preferred_element_type=jnp.float32)
    return (residual + branch_sum).astype(jnp.bfloat16)


def apply_layer(hidden_rows, norm_gain, route_ids, combine, gate_w, up_w, down_w, experts):
    normed_rows = rms_normed(hidden_rows, norm_gain)
    half_rows = hidden_rows.shape[0] // 2
    top_count = route_ids.shape[-1]
    capacity = max(2, min(half_rows, half_rows * top_count // experts * 3 // 2))
    grouped_routes = route_ids.reshape(2, half_rows, top_count)
    return mix_block(
        hidden_rows, normed_rows, grouped_routes, combine, gate_w, up_w, down_w, experts, capacity
    )


def local(in_flight, entering, norm_gain, w_gate, w_up, w_down, routes, combine_weight):
    section_index = lax.axis_index("section")
    experts = lax.axis_size("expert") * w_gate.shape[1]
    carried = in_flight[0]
    traced = []
    for tick_index in range(TICKS):
        layer_out = apply_layer(
            carried,
            norm_gain[0],
            routes[0, tick_index],
            combine_weight[0, tick_index],
            w_gate[0, 0],
            w_up[0, 0],
            w_down[0, 0],
            experts,
        )
        traced.append(layer_out)
        if tick_index + 1 < TICKS:
            shifted = passed_along(layer_out, "section", 1)
            carried = jnp.where(section_index == 0, entering[tick_index], shifted)
    return jnp.stack(traced)[:, None]


def solution(mesh):
    placed = (
        P("section", "expert", None),
        P(None, "expert", None),
        P("section", None),
        P("section", "expert", None, None),
        P("section", "expert", None, None),
        P("section", "expert", None, None),
        P("section", None, "expert", None),
        P("section", None, "expert", None),
    )
    return jax.shard_map(
        local,
        mesh=mesh,
        in_specs=placed,
        out_specs=P(None, "section", "expert", None),
        check_vma=False,
    )
```

profile of v0, /device:TPU:15, one launch (start us, length us, event | category | flops | bytes accessed | tf_op | source)
XLA Modules:
  0.0 370.5 jit_solution(13183694575999979211)
XLA Ops:
  0.0 0.0 copy-start
  0.0 0.9 fusion.56
  0.9 0.1 copy.30
  0.9 0.1 eq.115
  1.0 0.1 eq.111
  1.1 0.1 copy.31
  1.2 0.1 eq.130
  1.3 0.1 eq.126
  1.4 1.2 reduce-window.14
  2.6 0.2 slice_reduce_fusion.1
  2.8 0.1 fusion.49
  2.9 0.1 reshape.198
  3.1 1.2 reduce-window.16
  4.2 0.2 slice_reduce_fusion
  4.5 0.1 fusion.46
  4.6 0.1 reshape.204
  4.7 0.1 add.97
  4.8 0.1 add.98
  4.8 0.1 fusion.50
  4.9 0.5 convert_reduce_fusion.1
  5.5 0.7 mul.147
  6.2 1.1 fusion.26
  7.3 2.0 convolution_convert_fusion.3
  9.3 0.0 copy-start.7
  9.3 76.4 %all_to_all.20 = bf16[16,48,2048]{2,1,0:T(8,128)(2,1)S(1)} all-to-all(bf16[16,48,2048]{2,1,0:T(8,128)(2,1)S(1)} %bitcast.117), channel_id=1, replica_groups=mesh['section'=2,'expert'=16] {'expert'}, dimensions={0} | all-to-all | bytes 6291456 | tf_op jit(solution)/shard_map/all_to_all | solution.py:56
  85.7 0.0 copy-start.1
  85.7 1.7 copy-done.1
  87.4 0.0 copy-done.7
  87.4 4.0 %fusion.4 = f32[768,768]{1,0:T(8,128)} fusion(bf16[768,2048]{1,0:T(8,128)(2,1)S(1)} %bitcast.120, bf16[1,1,2048,768]{3,2,1,0:T(8,128)(2,1)S(1)} %copy-done.7), kind=kOutput, calls=%fused_computation.8 | convolution fusion | flops 2415919104 | bytes 8650752 | tf_op jit(solution)/shard_map/dot_general | solution.py:60
  91.4 0.0 copy-done
  91.4 11.0 %convolution_convert_fusion.2 = bf16[768,2048]{1,0:T(8,128)(2,1)} fusion(bf16[1,1,768,2048]{3,2,1,0:T(8,128)(2,1)S(1)} %copy-done, f32[768,768]{1,0:T(8,128)} %fusion.4, bf16[768,2048]{1,0:T(8,128)(2,1)} %bitcast.121, bf16[1,1,2048,768]{3,2,1,0:T(8,128)(2,1)} %param.11), kind=kOutput, calls=%fused_computation.2 | convolution fusion | flops 4836950016 | bytes 14942208 | tf_op jit(solution)/shard_map/dot_general | solution.py:62
  102.4 0.0 copy-start.6
  102.4 5.3 %all-to-all-start.1 = ((bf16[16,48,2048]{2,1,0:T(8,128)(2,1)}), bf16[16,48,2048]{2,1,0:T(8,128)(2,1)}, u32[]{:S(2)}, u32[]{:S(2)}) async-start(bf16[16,48,2048]{2,1,0:T(8,128)(2,1)} %bitcast.118), calls=%async_computation.1 | async-start | bytes 6291456 | tf_op jit(solution)/shard_map/all_to_all | solution.py:63
  107.8 0.0 copy-done.6
  107.8 0.0 copy-start.3
  107.8 0.1 copy.25
  107.9 1.2 select_reduce_fusion.1
  109.1 68.7 %all-to-all-done.1 = bf16[16,48,2048]{2,1,0:T(8,128)(2,1)} async-done(((bf16[16,48,2048]{2,1,0:T(8,128)(2,1)}), bf16[16,48,2048]{2,1,0:T(8,128)(2,1)}, u32[]{:S(2)}, u32[]{:S(2)}) %all-to-all-start.1) | async-done | bytes 3145760 | tf_op jit(solution)/shard_map/all_to_all | solution.py:63
  177.8 0.0 copy-start.5
  177.8 2.7 fusion.42
  180.4 0.0 copy-done.3
  180.5 0.0 copy-done.5
  180.5 3.3 fusion.12
  183.7 1.5 collective-permute-start
  185.2 0.5 convert_reduce_fusion
  185.7 7.9 %collective-permute-done = bf16[64,2048]{1,0:T(8,128)(2,1)} collective-permute-done((bf16[64,2048]{1,0:T(8,128)(2,1)}, bf16[64,2048]{1,0:T(8,128)(2,1)}, u32[]{:S(2)}, u32[]{:S(2)}) %collective-permute-start) | collective-permute-done | bytes 262176 | tf_op jit(solution)/shard_map/ppermute | solution.py:15
  193.6 1.2 fusion.23
  194.9 1.0 convolution_convert_fusion.1
  195.9 0.0 copy-start.8
  195.9 75.6 %all_to_all.21 = bf16[16,48,2048]{2,1,0:T(8,128)(2,1)S(1)} all-to-all(bf16[16,48,2048]{2,1,0:T(8,128)(2,1)S(1)} %bitcast.116), channel_id=1, replica_groups=mesh['section'=2,'expert'=16] {'expert'}, dimensions={0} | all-to-all | bytes 6291456 | tf_op jit(solution)/shard_map/all_to_all | solution.py:56
  271.5 0.0 copy-start.2
  271.5 1.7 copy-done.2
  273.2 0.0 copy-done.8
  273.2 4.0 %fusion.2 = f32[768,768]{1,0:T(8,128)} fusion(bf16[768,2048]{1,0:T(8,128)(2,1)S(1)} %bitcast.122, bf16[1,1,2048,768]{3,2,1,0:T(8,128)(2,1)S(1)} %copy-done.8), kind=kOutput, calls=%fused_computation.6 | convolution fusion | flops 2415919104 | bytes 8650752 | tf_op jit(solution)/shard_map/dot_general | solution.py:60
  277.2 11.0 %convolution_convert_fusion = bf16[768,2048]{1,0:T(8,128)(2,1)} fusion(bf16[1,1,768,2048]{3,2,1,0:T(8,128)(2,1)S(1)} %copy-done, f32[768,768]{1,0:T(8,128)} %fusion.2, bf16[768,2048]{1,0:T(8,128)(2,1)} %bitcast.123, bf16[1,1,2048,768]{3,2,1,0:T(8,128)(2,1)} %param.11), kind=kOutput, calls=%fused_computation | convolution fusion | flops 4836950016 | bytes 14942208 | tf_op jit(solution)/shard_map/dot_general | solution.py:62
  288.2 5.2 %all-to-all-start.3 = ((bf16[16,48,2048]{2,1,0:T(8,128)(2,1)}), bf16[16,48,2048]{2,1,0:T(8,128)(2,1)}, u32[]{:S(2)}, u32[]{:S(2)}) async-start(bf16[16,48,2048]{2,1,0:T(8,128)(2,1)} %bitcast.119), calls=%async_computation.3 | async-start | bytes 6291456 | tf_op jit(solution)/shard_map/all_to_all | solution.py:63
  293.4 0.1 copy.28
  293.5 1.2 select_reduce_fusion
  294.7 68.7 %all-to-all-done.3 = bf16[16,48,2048]{2,1,0:T(8,128)(2,1)} async-done(((bf16[16,48,2048]{2,1,0:T(8,128)(2,1)}), bf16[16,48,2048]{2,1,0:T(8,128)(2,1)}, u32[]{:S(2)}, u32[]{:S(2)}) %all-to-all-start.3) | async-done | bytes 3145760 | tf_op jit(solution)/shard_map/all_to_all | solution.py:63
  363.4 0.0 copy-start.4
  363.4 2.7 fusion.39
  366.1 0.0 copy-done.4
  366.1 2.6 fusion.14
  368.7 1.8 maximum_bitcast_fusion
  (10 shorter events, 0.1 us)
Async XLA Ops:
  0.0 91.4 %copy-start = (bf16[1,1,768,2048]{3,2,1,0:T(8,128)(2,1)S(1)}, bf16[1,1,768,2048]{3,2,1,0:T(8,128)(2,1)}, u32[]{:S(2)}) copy-start(bf16[1,1,768,2048]{3,2,1,0:T(8,128)(2,1)} %param.13) | copy-start | bytes 9437188
  9.3 78.1 %copy-start.7 = (bf16[1,1,2048,768]{3,2,1,0:T(8,128)(2,1)S(1)}, bf16[1,1,2048,768]{3,2,1,0:T(8,128)(2,1)}, u32[]{:S(2)}) copy-start(bf16[1,1,2048,768]{3,2,1,0:T(8,128)(2,1)} %param.12) | copy-start | bytes 9437188
  85.7 1.7 copy-start.1
  102.4 5.3 %copy-start.6 = (f32[1,2,64,8]{2,3,1,0:T(8,128)S(1)}, f32[1,2,64,8]{2,3,1,0:T(8,128)}, u32[]{:S(2)}) copy-start(f32[1,2,64,8]{2,3,1,0:T(8,128)} %param.15) | copy-start | bytes 12292
  102.4 75.3 %all-to-all-start.1 = ((bf16[16,48,2048]{2,1,0:T(8,128)(2,1)}), bf16[16,48,2048]{2,1,0:T(8,128)(2,1)}, u32[]{:S(2)}, u32[]{:S(2)}) async-start(bf16[16,48,2048]{2,1,0:T(8,128)(2,1)} %bitcast.118), calls=%async_computation.1 | async-start | bytes 6291456 | tf_op jit(solution)/shard_map/all_to_all | solution.py:63
  107.8 72.7 %copy-start.3 = (bf16[1,64,2048]{2,1,0:T(8,128)(2,1)S(1)}, bf16[1,64,2048]{2,1,0:T(8,128)(2,1)}, u32[]{:S(2)}) copy-start(bf16[1,64,2048]{2,1,0:T(8,128)(2,1)} %param.8) | copy-start | bytes 786436
  177.8 2.7 copy-start.5
  183.7 9.9 %collective-permute-start = (bf16[64,2048]{1,0:T(8,128)(2,1)}, bf16[64,2048]{1,0:T(8,128)(2,1)}, u32[]{:S(2)}, u32[]{:S(2)}) collective-permute-start(bf16[64,2048]{1,0:T(8,128)(2,1)} %fusion.12), channel_id=1, source_target_pairs={{0,16},{1,17},{2,18},{3,19},{4,20},{5,21},{6,22},{7,23},{8,24},{9,... | collective-permute-start | bytes 786440 | tf_op jit(solution)/shard_map/ppermute | solution.py:15
  195.9 77.3 %copy-start.8 = (bf16[1,1,2048,768]{3,2,1,0:T(8,128)(2,1)S(1)}, bf16[1,1,2048,768]{3,2,1,0:T(8,128)(2,1)}, u32[]{:S(2)}) copy-start(bf16[1,1,2048,768]{3,2,1,0:T(8,128)(2,1)} %param.12) | copy-start | bytes 9437188
  271.5 1.7 copy-start.2
  288.2 75.2 %all-to-all-start.3 = ((bf16[16,48,2048]{2,1,0:T(8,128)(2,1)}), bf16[16,48,2048]{2,1,0:T(8,128)(2,1)}, u32[]{:S(2)}, u32[]{:S(2)}) async-start(bf16[16,48,2048]{2,1,0:T(8,128)(2,1)} %bitcast.119), calls=%async_computation.3 | async-start | bytes 6291456 | tf_op jit(solution)/shard_map/all_to_all | solution.py:63
  363.4 2.7 copy-start.4
where the time goes:
time: 371 us; the launch traced here: 370 us
  blocking collectives  152 us (41%)
  waiting for transfers between devices  145 us (39%)
  matrix products  44.3 us (12%)
  starting transfers between devices  12 us (3%)
  other arithmetic  11 us (3%)
  local copies, waits for them, and re-layouts  5.79 us (2%)
    all_to_all x2, blocking collectives, mix_block(): lax.all_to_all(outgoing, 'expert', split_axis=0, concat_axis=0, tiled=True)  152 us
    all_to_all x2, waiting for transfers between devices, mix_block(): lax.all_to_all(result.reshape(row_shape), 'expert', split_axis=0, concat_...  137 us
    dot_general x2, matrix products, mix_block(): jnp.dot(hidden, down_w, preferred_element_type=jnp.float32)  22 us
    all_to_all x2, starting transfers between devices, mix_block(): lax.all_to_all(result.reshape(row_shape), 'expert', split_axis=0, concat_...  10.5 us
    dot_general x2, matrix products, mix_block(): up_sum = jnp.dot(inputs, up_w, preferred_element_type=jnp.float32)  8.06 us
    ppermute x1, waiting for transfers between devices, passed_along(): return lax.ppermute(x, axis, pairs)  7.89 us
  transfers between devices with their start and end apart: 3, of which 3 were waited for; matrix products, arithmetic and copies ran while one was open for 1% of the time, Pallas kernels for 0%

commit v1 on v0

v1 whole, which is shorter than its diff:
```python
import jax
import jax.numpy as jnp
from jax import lax
from jax.sharding import PartitionSpec as P

TICKS = 2
EPSILON = 1e-06


def passed_along(x, axis, by):
    devices = lax.axis_size(axis)
    pairs = [(i, i + by) for i in range(devices) if 0 <= i + by < devices]
    return lax.ppermute(x, axis, pairs)


def rms_normed(hidden_rows, norm_gain):
    as_float = hidden_rows.astype(jnp.float32)
    inv_scale = lax.rsqrt(jnp.mean(as_float * as_float, axis=-1, keepdims=True) + EPSILON)
    return (as_float * inv_scale * norm_gain.astype(jnp.float32)).astype(jnp.bfloat16)


def expert_weights(routes, combine, experts):
    hits = routes[..., None] == jnp.arange(experts, dtype=jnp.int32)
    return jnp.sum(jnp.where(hits, combine[..., None], 0.0), axis=-2)


def gathered_layer(hidden_rows, norm_gain, scales, gate_w, up_w, down_w):
    normed = rms_normed(hidden_rows, norm_gain)
    inputs = lax.all_gather(normed, "expert", axis=0, tiled=True)
    gate_sum = jnp.dot(inputs, gate_w, preferred_element_type=jnp.float32)
    up_sum = jnp.dot(inputs, up_w, preferred_element_type=jnp.float32)
    hidden = (jax.nn.silu(gate_sum) * up_sum).astype(jnp.bfloat16)
    result = jnp.dot(hidden, down_w, preferred_element_type=jnp.float32)
    scaled = (result * scales).astype(jnp.bfloat16)
    summed = lax.psum_scatter(scaled, "expert", scatter_dimension=0, tiled=True)
    return (hidden_rows.astype(jnp.float32) + summed.astype(jnp.float32)).astype(jnp.bfloat16)


def local(in_flight, entering, norm_gain, w_gate, w_up, w_down, routes, combine_weight):
    section_index = lax.axis_index("section")
    experts = lax.axis_size("expert") * w_gate.shape[1]
    spread = expert_weights(routes[0], combine_weight[0], experts)
    mine = lax.all_to_all(spread, "expert", split_axis=2, concat_axis=1, tiled=True)
    carried = in_flight[0]
    traced = []
    for tick_index in range(TICKS):
        layer_out = gathered_layer(
            carried, norm_gain[0], mine[tick_index], w_gate[0, 0], w_up[0, 0], w_down[0, 0]
        )
        traced.append(layer_out)
        if tick_index + 1 < TICKS:
            shifted = passed_along(layer_out, "section", 1)
            carried = jnp.where(section_index == 0, entering[tick_index], shifted)
    return jnp.stack(traced)[:, None]


def solution(mesh):
    placed = (
        P("section", "expert", None),
        P(None, "expert", None),
        P("section", None),
        P("section", "expert", None, None),
        P("section", "expert", None, None),
        P("section", "expert", None, None),
        P("section", None, "expert", None),
        P("section", None, "expert", None),
    )
    return jax.shard_map(
        local,
        mesh=mesh,
        in_specs=placed,
        out_specs=P(None, "section", "expert", None),
        check_vma=False,
    )
```

time: 371 us -> 320 us (0.86)
  blocking collectives: 152 us -> 10.1 us
  waiting for transfers between devices: 145 us -> 237 us
  between operations: 0.22 us -> 13.2 us
  starting transfers between devices: 12 us -> 1.59 us
  local copies, waits for them, and re-layouts: 5.79 us -> 0.9 us
    all_to_all x2 -> x1, blocking collectives: 152 us -> 10.1 us  [local(): lax.all_to_all(spread, 'expert', split_axis=2, concat_axis=1, tiled=True)]
    reduce_scatter x0 -> x2, waiting for transfers between devices: none -> 139 us  [gathered_layer(): summed = lax.psum_scatter(scaled, 'expert', scatter_dimension=0, tiled=True)]
    all_to_all x2 -> x0, waiting for transfers between devices: 137 us -> none  [mix_block(): lax.all_to_all(result.reshape(row_shape), 'expert', split_axis=0, concat_...]
    all_gather x0 -> x2, waiting for transfers between devices: none -> 91.7 us  [gathered_layer(): inputs = lax.all_gather(normed, 'expert', axis=0, tiled=True)]
    all_to_all x2 -> x0, starting transfers between devices: 10.5 us -> none  [mix_block(): lax.all_to_all(result.reshape(row_shape), 'expert', split_axis=0, concat_...]
    convert_element_type x2 -> x3, other arithmetic: 0.01 us -> 4.34 us  [the longest x2 2.63 us: rms_normed(): (as_float * inv_scale * norm_gain.astype(jnp.float32)).astype(jnp.bfloat16)]
    dot_general x10 -> x4, matrix products: 44.3 us -> 41.3 us  [the longest x2 24.6 us: gathered_layer(): result = jnp.dot(hidden, down_w, preferred_element_type=jnp.float32)]
  transfers between devices with their start and end apart: 3 -> 5, of which waited for: 3 -> 5; matrix products, arithmetic and copies ran while one was open for 1% -> 1% of each run, Pallas kernels for 0% -> 0%
where the time goes in v1:
time: 320 us; the launch traced here: 316 us
  waiting for transfers between devices  237 us (74%)
  matrix products  41.3 us (13%)
  between operations  13.2 us (4%)
  other arithmetic  11.7 us (4%)
  blocking collectives  10.1 us (3%)
    reduce_scatter x2, waiting for transfers between devices, gathered_layer(): summed = lax.psum_scatter(scaled, 'expert', scatter_dimension=0, tiled=True)  139 us
    all_gather x2, waiting for transfers between devices, gathered_layer(): inputs = lax.all_gather(normed, 'expert', axis=0, tiled=True)  91.7 us
    dot_general x2, matrix products, gathered_layer(): result = jnp.dot(hidden, down_w, preferred_element_type=jnp.float32)  24.6 us
    dot_general x2, matrix products, gathered_layer(): up_sum = jnp.dot(inputs, up_w, preferred_element_type=jnp.float32)  16.7 us
    all_to_all x1, blocking collectives, local(): lax.all_to_all(spread, 'expert', split_axis=2, concat_axis=1, tiled=True)  10.1 us
  transfers between devices with their start and end apart: 5, of which 5 were waited for; matrix products, arithmetic and copies ran while one was open for 1% of the time, Pallas kernels for 0%

profile of v1, /device:TPU:15, one launch (start us, length us, event | category | flops | bytes accessed | tf_op | source)
XLA Modules:
  0.0 316.1 jit_solution(13919200037820988480)
XLA Ops:
  6.5 0.0 copy-start
  6.5 0.0 all-gather.3.cloned.1.call-start
  6.5 1.3 fusion.22
  7.8 0.7 mul.95
  8.5 1.8 fusion.24
  10.3 0.0 all-gather.3.cloned.1.call-update
  10.3 0.0 reduce-scatter.3.cloned.1.call-start
  10.4 0.7 select_reduce_fusion
  11.1 0.1 reshape.40
  11.2 10.1 %all_to_all.15 = f32[16,1,128]{2,1,0:T(1,128)S(1)} all-to-all(f32[16,1,128]{2,1,0:T(1,128)S(1)} %reshape.40), channel_id=1, replica_groups=mesh['section'=2,'expert'=16] {'expert'}, dimensions={0} | all-to-all | bytes 16384 | tf_op jit(solution)/shard_map/all_to_all | solution.py:43
  21.4 0.5 broadcast.43
  21.9 0.6 reduce.8
  22.5 0.1 reshape.41
  22.7 0.1 mul.83
  22.7 38.9 %all-gather.3.cloned.1.call-done = bf16[1024,2048]{1,0:T(8,128)(2,1)} async-done(((bf16[64,2048]{1,0:T(8,128)(2,1)}), bf16[1024,2048]{1,0:T(8,128)(2,1)}) %all-gather.3.cloned.1.call-update) | async-done | bytes 4194320 | tf_op jit(solution)/shard_map/all_gather | solution.py:29
  61.7 8.3 %fusion.4 = f32[1024,768]{1,0:T(8,128)} fusion(bf16[1024,2048]{1,0:T(8,128)(2,1)} %all-gather.3.cloned.1.call-done, bf16[1,1,2048,768]{3,2,1,0:T(8,128)(2,1)} %param.12), kind=kOutput, calls=%fused_computation.6 | convolution fusion | flops 3221225472 | bytes 10485760 | tf_op jit(solution)/shard_map/dot_general | solution.py:31
  70.0 0.0 copy-done
  70.0 12.3 %multiply_convert_fusion.1 = bf16[1024,2048]{1,0:T(8,128)(2,1)} fusion(f32[1024]{0:T(1024)S(1)} %mul.83, bf16[1,1,768,2048]{3,2,1,0:T(8,128)(2,1)S(1)} %copy-done, f32[1024,768]{1,0:T(8,128)} %fusion.4, bf16[1024,2048]{1,0:T(8,128)(2,1)} %all-gather.3.cloned.1.call-done, bf16[1,1,2048,768]{3,2,1,0:T(8,128)(2,1)} %param.11), kind=kOutput, calls=%fused_computation.1 | convolution fusion | flops 6451363840 | bytes 17829888 | tf_op jit(solution)/shard_map/dot_general | solution.py:33
  82.3 0.0 copy-start.1
  82.3 0.0 reduce-scatter.3.cloned.1.call-update
  82.4 0.0 all-gather.5.cloned.1.call-start
  82.4 69.5 %reduce-scatter.3.cloned.1.call-done = bf16[64,2048]{1,0:T(8,128)(2,1)} async-done(((bf16[1024,2048]{1,0:T(8,128)(2,1)}), bf16[64,2048]{1,0:T(8,128)(2,1)}) %reduce-scatter.3.cloned.1.call-update) | async-done | bytes 262160 | tf_op jit(solution)/shard_map/reduce_scatter | solution.py:35
  151.9 0.0 copy-done.1
  151.9 1.7 fusion.25
  153.6 1.3 collective-permute-start
  154.9 6.1 %collective-permute-done = bf16[64,2048]{1,0:T(8,128)(2,1)} collective-permute-done((bf16[64,2048]{1,0:T(8,128)(2,1)}, bf16[64,2048]{1,0:T(8,128)(2,1)}, u32[]{:S(2)}, u32[]{:S(2)}) %collective-permute-start) | collective-permute-done | bytes 262176 | tf_op jit(solution)/shard_map/ppermute | solution.py:13
  161.1 1.2 fusion.18
  162.3 0.8 fusion.20
  163.2 0.0 all-gather.5.cloned.1.call-update
  163.2 0.2 reduce-scatter.5.cloned.1.call-start
  163.4 0.1 mul.92
  163.5 52.8 %all-gather.5.cloned.1.call-done = bf16[1024,2048]{1,0:T(8,128)(2,1)} async-done(((bf16[64,2048]{1,0:T(8,128)(2,1)}), bf16[1024,2048]{1,0:T(8,128)(2,1)}) %all-gather.5.cloned.1.call-update) | async-done | bytes 4194320 | tf_op jit(solution)/shard_map/all_gather | solution.py:29
  216.3 8.3 %fusion.2 = f32[1024,768]{1,0:T(8,128)} fusion(bf16[1024,2048]{1,0:T(8,128)(2,1)} %all-gather.5.cloned.1.call-done, bf16[1,1,2048,768]{3,2,1,0:T(8,128)(2,1)} %param.12), kind=kOutput, calls=%fused_computation.4 | convolution fusion | flops 3221225472 | bytes 10485760 | tf_op jit(solution)/shard_map/dot_general | solution.py:31
  224.6 12.3 %multiply_convert_fusion = bf16[1024,2048]{1,0:T(8,128)(2,1)} fusion(f32[1024]{0:T(1024)S(1)} %mul.92, bf16[1,1,768,2048]{3,2,1,0:T(8,128)(2,1)S(1)} %copy-done, f32[1024,768]{1,0:T(8,128)} %fusion.2, bf16[1024,2048]{1,0:T(8,128)(2,1)} %all-gather.5.cloned.1.call-done, bf16[1,1,2048,768]{3,2,1,0:T(8,128)(2,1)} %param.11), kind=kOutput, calls=%fused_computation | convolution fusion | flops 6451363840 | bytes 17829888 | tf_op jit(solution)/shard_map/dot_general | solution.py:33
  236.9 0.0 reduce-scatter.5.cloned.1.call-update
  236.9 69.8 %reduce-scatter.5.cloned.1.call-done = bf16[64,2048]{1,0:T(8,128)(2,1)} async-done(((bf16[1024,2048]{1,0:T(8,128)(2,1)}), bf16[64,2048]{1,0:T(8,128)(2,1)}) %reduce-scatter.5.cloned.1.call-update) | async-done | bytes 262160 | tf_op jit(solution)/shard_map/reduce_scatter | solution.py:35
  306.7 1.0 fusion.26
  307.7 1.8 maximum_bitcast_fusion
  (5 shorter events, 0.1 us)
Async XLA Ops:
  6.5 63.5 %copy-start = (bf16[1,1,768,2048]{3,2,1,0:T(8,128)(2,1)S(1)}, bf16[1,1,768,2048]{3,2,1,0:T(8,128)(2,1)}, u32[]{:S(2)}) copy-start(bf16[1,1,768,2048]{3,2,1,0:T(8,128)(2,1)} %param.13) | copy-start | bytes 9437188
  6.5 55.1 %all-gather.3.cloned.1.call-start = ((), (), s32[]{:S(2)}) async-start(), calls=%async_computation.3 | async-start | bytes 4456448 | tf_op jit(solution)/shard_map/all_gather | solution.py:29
  10.3 141.6 %reduce-scatter.3.cloned.1.call-start = ((), (), s32[]{:S(2)}) async-start(), calls=%async_computation.4 | async-start | bytes 4456448 | tf_op jit(solution)/shard_map/reduce_scatter | solution.py:35
  82.3 69.6 %copy-start.1 = (bf16[1,64,2048]{2,1,0:T(8,128)(2,1)S(1)}, bf16[1,64,2048]{2,1,0:T(8,128)(2,1)}, u32[]{:S(2)}) copy-start(bf16[1,64,2048]{2,1,0:T(8,128)(2,1)} %param.8) | copy-start | bytes 786436
  82.4 133.9 %all-gather.5.cloned.1.call-start = ((), (), s32[]{:S(2)}) async-start(), calls=%async_computation.5 | async-start | bytes 4456448 | tf_op jit(solution)/shard_map/all_gather | solution.py:29
  153.6 7.4 %collective-permute-start = (bf16[64,2048]{1,0:T(8,128)(2,1)}, bf16[64,2048]{1,0:T(8,128)(2,1)}, u32[]{:S(2)}, u32[]{:S(2)}) collective-permute-start(bf16[64,2048]{1,0:T(8,128)(2,1)} %fusion.25), channel_id=1, source_target_pairs={{0,16},{1,17},{2,18},{3,19},{4,20},{5,21},{6,22},{7,23},{8,24},{9,... | collective-permute-start | bytes 786440 | tf_op jit(solution)/shard_map/ppermute | solution.py:13
  163.2 143.5 %reduce-scatter.5.cloned.1.call-start = ((), (), s32[]{:S(2)}) async-start(), calls=%async_computation.6 | async-start | bytes 4456448 | tf_op jit(solution)/shard_map/reduce_scatter | solution.py:35
Sparse Core Ops, SparseCore 0:
  10.5 51.1 all-gather.2
  82.5 69.4 reduce-scatter.2
  163.3 52.9 all-gather.4
  237.1 69.6 reduce-scatter.4

commit v2 on v1

--- a/solution.py
+++ b/solution.py
@@ -1,6 +1,8 @@
 import jax
 import jax.numpy as jnp
 from jax import lax
+from jax.experimental import pallas as pl
+from jax.experimental.pallas import tpu as pltpu
 from jax.sharding import PartitionSpec as P
 
 TICKS = 2
@@ -36,11 +38,223 @@
     return (hidden_rows.astype(jnp.float32) + summed.astype(jnp.float32)).astype(jnp.bfloat16)
 
 
+NZ = 4
+
+
+def layers_kernel(
+    x_ref, entering_ref, gain_ref, scale_ref, gate_hbm, up_hbm, down_hbm, out_ref,
+    gathered, held_next, hidden, part, core_in, chip_sum, x_in, pair_sum, z_in,
+    gate_w, up_w, down_w,
+    w_sem, zs, zr, xs, xr, cs, cr, ps, pr, qs, qr, ts, tr, hs, hr,
+):
+    section = lax.axis_index("section")
+    me = lax.axis_index("expert")
+    core = me % 2
+    across = (me // 2) % 2
+    z = me // 4
+    zpeer = [z, z + 1 - 2 * (z % 2), (z + 2) % 4, 3 - z]
+
+    def expert_id(zz, xx, cc):
+        return {"expert": zz * 4 + xx * 2 + cc}
+
+    z_ids = [expert_id(zpeer[d], across, core) for d in range(NZ)]
+    x_id = expert_id(z, 1 - across, core)
+    c_id = expert_id(z, across, 1 - core)
+    s_id = {"section": 1 - section}
+
+    loads = [
+        pltpu.make_async_copy(src, dst, w_sem.at[i])
+        for i, (src, dst) in enumerate(((gate_hbm, gate_w), (up_hbm, up_w), (down_hbm, down_w)))
+    ]
+    for load in loads:
+        load.start()
+
+    barrier = pltpu.get_barrier_semaphore()
+    for peer in z_ids[1:] + [x_id, c_id, s_id]:
+        pl.semaphore_signal(barrier, inc=1, device_id=peer, device_id_type=pl.DeviceIdType.MESH)
+
+    sends = []
+
+    def send(src, dst, s_sem, r_sem, peer):
+        copy = pltpu.make_async_remote_copy(
+            src_ref=src, dst_ref=dst, send_sem=s_sem, recv_sem=r_sem,
+            device_id=peer, device_id_type=pl.DeviceIdType.MESH,
+        )
+        copy.start()
+        sends.append(copy)
+
+    def arrived(ref, s_sem, r_sem, peer):
+        pltpu.make_async_remote_copy(
+            src_ref=ref, dst_ref=ref, send_sem=s_sem, recv_sem=r_sem,
+            device_id=peer, device_id_type=pl.DeviceIdType.MESH,
+        ).wait_recv()
+
+    def run_tick(t, first):
+        rows = x_ref[...] if t == 0 else held_next[...]
+        as_float = rows.astype(jnp.float32)
+        inv = lax.rsqrt(jnp.mean(as_float * as_float, axis=-1, keepdims=True) + EPSILON)
+        own = gathered.at[t, z, across, core]
+        own[...] = (as_float * inv * gain_ref[...].astype(jnp.float32)).astype(jnp.bfloat16)
+        if first:
+            pl.semaphore_wait(barrier, NZ + 2)
+        for d in range(1, NZ):
+            send(own, own, zs.at[t, d], zr.at[t, d], z_ids[d])
+
+        def stage_a(k):
+            mine = gathered.at[t, zpeer[k], across, core]
+            if k:
+                arrived(mine, zs.at[t, k], zr.at[t, k], z_ids[k])
+            send(mine, mine, xs.at[t, k], xr.at[t, k], x_id)
+            send(mine, mine, cs.at[t, 0, k], cr.at[t, 0, k], c_id)
+
+        def stage_b(k):
+            other = gathered.at[t, zpeer[k], 1 - across, core]
+            arrived(other, xs.at[t, k], xr.at[t, k], x_id)
+            send(other, other, cs.at[t, 1, k], cr.at[t, 1, k], c_id)
+
+        def stage_c(k):
+            arrived(gathered.at[t, zpeer[k], across, 1 - core], cs.at[t, 0, k], cr.at[t, 0, k], c_id)
+            arrived(
+                gathered.at[t, zpeer[k], 1 - across, 1 - core], cs.at[t, 1, k], cr.at[t, 1, k], c_id
+            )
+            if first and k == 0:
+                for load in loads:
+                    load.wait()
+            group = gathered.at[t, zpeer[k]]
+            count = 4 * group.shape[2]
+            height = group.shape[2]
+
+            def up_tile(i, carry):
+                columns = pl.ds(pl.multiple_of(i * 256, 256), 256)
+                inputs = group[...].reshape(count, group.shape[3])
+                g = jnp.dot(inputs, gate_w[:, columns], preferred_element_type=jnp.float32)
+                u = jnp.dot(inputs, up_w[:, columns], preferred_element_type=jnp.float32)
+                hidden[:, columns] = (g / (1.0 + jnp.exp(-g)) * u).astype(jnp.bfloat16)
+                return carry
+
+            lax.fori_loop(0, hidden.shape[1] // 256, up_tile, 0)
+            start = pl.multiple_of(zpeer[k] * count, count)
+            scale = scale_ref[t, pl.ds(start, count), :]
+
+            def down_tile(i, carry):
+                columns = pl.ds(pl.multiple_of(i * 256, 256), 256)
+                r = jnp.dot(hidden[...], down_w[:, columns], preferred_element_type=jnp.float32)
+                r = (r * scale).astype(jnp.bfloat16)
+                for xx in range(2):
+                    for cc in range(2):
+                        at = (xx * 2 + cc) * height
+                        part[t, k, cc, xx, :, columns] = r[at : at + height]
+                return carry
+
+            lax.fori_loop(0, down_w.shape[1] // 256, down_tile, 0)
+            send(part.at[t, k, 1 - core], core_in.at[t, k], ps.at[t, k], pr.at[t, k], c_id)
+
+        def stage_d(k):
+            arrived(core_in.at[t, k], ps.at[t, k], pr.at[t, k], c_id)
+            chip_sum[t, k] = (
+                part[t, k, core].astype(jnp.float32) + core_in[t, k].astype(jnp.float32)
+            ).astype(jnp.bfloat16)
+            send(chip_sum.at[t, k, 1 - across], x_in.at[t, k], qs.at[t, k], qr.at[t, k], x_id)
+
+        def stage_e(k):
+            arrived(x_in.at[t, k], qs.at[t, k], qr.at[t, k], x_id)
+            pair_sum[t, k] = (
+                chip_sum[t, k, across].astype(jnp.float32) + x_in[t, k].astype(jnp.float32)
+            ).astype(jnp.bfloat16)
+            if k:
+                send(pair_sum.at[t, k], z_in.at[t, k], ts.at[t, k], tr.at[t, k], z_ids[k])
+
+        for step in range(NZ + 4):
+            for lag, stage in ((0, stage_a), (1, stage_b), (3, stage_d), (4, stage_e), (2, stage_c)):
+                if 0 <= step - lag < NZ:
+                    stage(step - lag)
+
+        total = as_float + pair_sum[t, 0].astype(jnp.float32)
+        for k in range(1, NZ):
+            arrived(z_in.at[t, k], ts.at[t, k], tr.at[t, k], z_ids[k])
+            total = total + z_in[t, k].astype(jnp.float32)
+        out_ref[t] = total.astype(jnp.bfloat16)
+
+    run_tick(0, True)
+    carry = pltpu.make_async_remote_copy(
+        src_ref=out_ref.at[0], dst_ref=held_next, send_sem=hs, recv_sem=hr,
+        device_id=s_id, device_id_type=pl.DeviceIdType.MESH,
+    )
+
+    @pl.when(section == 0)
+    def _():
+        carry.start()
+        held_next[...] = entering_ref[...]
+
+    @pl.when(section == 1)
+    def _():
+        carry.wait_recv()
+
+    run_tick(1, False)
+
+    @pl.when(section == 0)
+    def _():
+        carry.wait_send()
+
+    for copy in sends:
+        copy.wait_send()
+
+
+def layers_call(held, entering, gain, scales, gate_w, up_w, down_w):
+    rows, width = held.shape
+    inner = gate_w.shape[1]
+    bf16 = jnp.bfloat16
+    dma = pltpu.SemaphoreType.DMA
+    vmem = pl.BlockSpec(memory_space=pltpu.VMEM)
+    hbm = pl.BlockSpec(memory_space=pl.ANY)
+    tall = TICKS * 16 * rows
+    return pl.pallas_call(
+        layers_kernel,
+        out_shape=jax.ShapeDtypeStruct((TICKS, rows, width), bf16),
+        in_specs=[vmem] * 4 + [hbm] * 3,
+        out_specs=vmem,
+        scratch_shapes=[
+            pltpu.VMEM((TICKS, NZ, 2, 2, rows, width), bf16),
+            pltpu.VMEM((rows, width), bf16),
+            pltpu.VMEM((4 * rows, inner), bf16),
+            pltpu.VMEM((TICKS, NZ, 2, 2, rows, width), bf16),
+            pltpu.VMEM((TICKS, NZ, 2, rows, width), bf16),
+            pltpu.VMEM((TICKS, NZ, 2, rows, width), bf16),
+            pltpu.VMEM((TICKS, NZ, rows, width), bf16),
+            pltpu.VMEM((TICKS, NZ, rows, width), bf16),
+            pltpu.VMEM((TICKS, NZ, rows, width), bf16),
+            pltpu.VMEM(gate_w.shape, bf16),
+            pltpu.VMEM(up_w.shape, bf16),
+            pltpu.VMEM(down_w.shape, bf16),
+            dma((3,)),
+            dma((TICKS, NZ)), dma((TICKS, NZ)),
+            dma((TICKS, NZ)), dma((TICKS, NZ)),
+            dma((TICKS, 2, NZ)), dma((TICKS, 2, NZ)),
+            dma((TICKS, NZ)), dma((TICKS, NZ)),
+            dma((TICKS, NZ)), dma((TICKS, NZ)),
+            dma((TICKS, NZ)), dma((TICKS, NZ)),
+            dma, dma,
+        ],
+        compiler_params=pltpu.CompilerParams(
+            collective_id=0, has_side_effects=True, vmem_limit_bytes=58 * 2**20
+        ),
+        cost_estimate=pl.CostEstimate(
+            flops=6 * tall * width * inner,
+            bytes_accessed=6 * width * inner + 8 * rows * width,
+            transcendentals=tall * inner,
+        ),
+    )(held, entering, gain, scales, gate_w, up_w, down_w)
+
+
 def local(in_flight, entering, norm_gain, w_gate, w_up, w_down, routes, combine_weight):
     section_index = lax.axis_index("section")
     experts = lax.axis_size("expert") * w_gate.shape[1]
     spread = expert_weights(routes[0], combine_weight[0], experts)
     mine = lax.all_to_all(spread, "expert", split_axis=2, concat_axis=1, tiled=True)
+    if experts == 4 * NZ and lax.axis_size("section") == 2:
+        return layers_call(
+            in_flight[0], entering[0], norm_gain, mine, w_gate[0, 0], w_up[0, 0], w_down[0, 0]
+        )[:, None]
     carried = in_flight[0]
     traced = []
     for tick_index in range(TICKS):

time: 320 us -> 179 us (0.56)
  waiting for transfers between devices: 237 us -> 0 us
  Pallas kernels: 0 us -> 161 us
  matrix products: 41.3 us -> 0 us
  between operations: 13.2 us -> 0.03 us
  other arithmetic: 11.7 us -> 1.41 us
  local copies, waits for them, and re-layouts: 0.9 us -> 4.58 us
    pallas_call x0 -> x1, Pallas kernels: none -> 161 us  [layers_call(): pl.pallas_call(layers_kernel, out_shape=jax.ShapeDtypeStruct((TICKS, rows...]
    reduce_scatter x2 -> x0, waiting for transfers between devices: 139 us -> none  [gathered_layer(): summed = lax.psum_scatter(scaled, 'expert', scatter_dimension=0, tiled=True)]
    all_gather x2 -> x0, waiting for transfers between devices: 91.7 us -> none  [gathered_layer(): inputs = lax.all_gather(normed, 'expert', axis=0, tiled=True)]
    dot_general x4 -> x0, matrix products: 41.3 us -> none  [the longest x2 24.6 us: gathered_layer(): result = jnp.dot(hidden, down_w, preferred_element_type=jnp.float32)]
    ppermute x1 -> x0, waiting for transfers between devices: 6.13 us -> none  [passed_along(): return lax.ppermute(x, axis, pairs)]
    convert_element_type x3 -> x0, other arithmetic: 4.34 us -> none  [the longest x2 2.63 us: rms_normed(): (as_float * inv_scale * norm_gain.astype(jnp.float32)).astype(jnp.bfloat16)]
  transfers between devices with their start and end apart: 5 -> 0, of which waited for: 5 -> 0; matrix products, arithmetic and copies ran while one was open for 1% -> 0% of each run, Pallas kernels for 0% -> 0%
where the time goes in v2:
time: 179 us; the launch traced here: 177 us
  Pallas kernels  161 us (90%)
  blocking collectives  10.1 us (6%)
  local copies, waits for them, and re-layouts  4.58 us (3%)
    pallas_call x1, Pallas kernels, layers_call(): pl.pallas_call(layers_kernel, out_shape=jax.ShapeDtypeStruct((TICKS, rows...  161 us
    all_to_all x1, blocking collectives, local(): lax.all_to_all(spread, 'expert', split_axis=2, concat_axis=1, tiled=True)  10.1 us

profile of v2, /device:TPU:15, one launch (start us, length us, event | category | flops | bytes accessed | tf_op | source)
XLA Modules:
  0.0 177.0 jit_solution(15058829739837345845)
XLA Ops:
  0.0 0.7 select_reduce_fusion
  0.8 0.1 reshape.2
  0.9 10.1 %all_to_all.19 = f32[16,1,128]{2,1,0:T(1,128)S(1)} all-to-all(f32[16,1,128]{2,1,0:T(1,128)S(1)} %reshape.2), channel_id=1, replica_groups=mesh['section'=2,'expert'=16] {'expert'}, dimensions={0} | all-to-all | bytes 16384 | tf_op jit(solution)/shard_map/all_to_all | solution.py:253
  11.0 0.5 broadcast
  11.5 0.7 reduce
  12.2 0.1 reshape.3
  12.3 2.0 %all_to_all.17.scale_ref = f32[2,1024,1]{2,1,0:T(8,128)} reshape(f32[2,16,64,1]{2,1,0,3:T(8,128)S(1)} %copy.22) | data formatting | bytes 16384 | tf_op jit(solution)/shard_map/all_to_all | solution.py:253
  14.3 160.9 %shard_map.82 = bf16[2,64,2048]{2,1,0:T(8,128)(2,1)} custom-call(bf16[64,2048]{1,0:T(8,128)(2,1)} %bitcast.30, bf16[64,2048]{1,0:T(8,128)(2,1)} %bitcast.31, bf16[1,2048]{1,0:T(2,128)(2,1)} %gain_ref.1, f32[2,1024,1]{2,1,0:T(8,128)} %all_to_all.17.scale_ref, bf16[2048,768]{1,0:T(8,128)(2,1)} %bitcast.27, bf16[2048,768]{1,0:T(8,128)(2,1)} %bitcast.28, ...), custom_call_target="tpu_custom_call" | custom-call | flops 19327352832 | bytes 10485760 | tf_op jit(solution)/shard_map/pallas_call | solution.py:211
  175.1 1.9 %copy.28 = bf16[2,1,64,2048]{3,2,1,0:T(8,128)(2,1)} copy(bf16[2,1,64,2048]{3,2,1,0:T(8,128)(2,1)} %bitcast.23) | data formatting | bytes 1048576
  (3 shorter events, 0.0 us)

commit v3 on v2

--- a/solution.py
+++ b/solution.py
@@ -42,17 +42,26 @@
 
 
 def layers_kernel(
-    x_ref, entering_ref, gain_ref, scale_ref, gate_hbm, up_hbm, down_hbm, out_ref,
+    x_ref, entering_ref, gain_ref, spread_ref, gate_hbm, up_hbm, down_hbm, out_ref,
     gathered, held_next, hidden, part, core_in, chip_sum, x_in, pair_sum, z_in,
-    gate_w, up_w, down_w,
-    w_sem, zs, zr, xs, xr, cs, cr, ps, pr, qs, qr, ts, tr, hs, hr,
+    gate_w, up_w, down_w, spread_in, scale_ref,
+    w_sem, ss, sr, zs, zr, xs, xr, cs, cr, ps, pr, qs, qr, ts, tr, hs, hr,
 ):
     section = lax.axis_index("section")
     me = lax.axis_index("expert")
     core = me % 2
     across = (me // 2) % 2
     z = me // 4
-    zpeer = [z, z + 1 - 2 * (z % 2), (z + 2) % 4, 3 - z]
+    inner = ((z + 1) // 2) % 2
+    near, skip, mirror = z + 1 - 2 * (z % 2), (z + 2) % 4, 3 - z
+    zpeer = [
+        z,
+        near,
+        (1 - inner) * skip + inner * mirror,
+        (1 - inner) * mirror + inner * skip,
+    ]
+    lane = [0, 1, 2 + inner, 3 - inner]
+    devices = 4 * NZ
 
     def expert_id(zz, xx, cc):
         return {"expert": zz * 4 + xx * 2 + cc}
@@ -70,18 +79,34 @@
         load.start()
 
     barrier = pltpu.get_barrier_semaphore()
-    for peer in z_ids[1:] + [x_id, c_id, s_id]:
+    others = [{"expert": (me + d) % devices} for d in range(1, devices)]
+    for peer in others + [s_id]:
         pl.semaphore_signal(barrier, inc=1, device_id=peer, device_id_type=pl.DeviceIdType.MESH)
+    spread_in[me] = spread_ref[me]
 
     sends = []
-
-    def send(src, dst, s_sem, r_sem, peer):
-        copy = pltpu.make_async_remote_copy(
+    inner_sends = []
+
+    def describe(src, dst, s_sem, r_sem, peer):
+        return pltpu.make_async_remote_copy(
             src_ref=src, dst_ref=dst, send_sem=s_sem, recv_sem=r_sem,
             device_id=peer, device_id_type=pl.DeviceIdType.MESH,
         )
+
+    def begin(*args):
+        copy = describe(*args)
         copy.start()
-        sends.append(copy)
+        return copy
+
+    def send(*args):
+        sends.append(begin(*args))
+
+    def send_inner(*args):
+        @pl.when(inner == 1)
+        def _():
+            begin(*args)
+
+        inner_sends.append(args)
 
     def arrived(ref, s_sem, r_sem, peer):
         pltpu.make_async_remote_copy(
@@ -96,16 +121,25 @@
         own = gathered.at[t, z, across, core]
         own[...] = (as_float * inv * gain_ref[...].astype(jnp.float32)).astype(jnp.bfloat16)
         if first:
-            pl.semaphore_wait(barrier, NZ + 2)
-        for d in range(1, NZ):
-            send(own, own, zs.at[t, d], zr.at[t, d], z_ids[d])
+            pl.semaphore_wait(barrier, devices)
+        send(own, own, zs.at[t, 0], zr.at[t, 1], z_ids[1])
+        send_inner(own, own, zs.at[t, 1], zr.at[t, 2], z_ids[2])
 
         def stage_a(k):
             mine = gathered.at[t, zpeer[k], across, core]
             if k:
-                arrived(mine, zs.at[t, k], zr.at[t, k], z_ids[k])
+                arrived(mine, zs.at[t, 0], zr.at[t, k], z_ids[k])
+                if k == 1:
+                    send_inner(mine, mine, zs.at[t, 2], zr.at[t, 3], z_ids[2])
+                else:
+                    send_inner(mine, mine, zs.at[t, k + 1], zr.at[t, k], z_ids[1])
             send(mine, mine, xs.at[t, k], xr.at[t, k], x_id)
             send(mine, mine, cs.at[t, 0, k], cr.at[t, 0, k], c_id)
+
+            if first and k == 0:
+                for d in range(1, devices):
+                    peer = (me + d) % devices
+                    send(spread_ref.at[peer], spread_in.at[me], ss.at[d], sr.at[d], {"expert": peer})
 
         def stage_b(k):
             other = gathered.at[t, zpeer[k], 1 - across, core]
@@ -118,6 +152,16 @@
                 gathered.at[t, zpeer[k], 1 - across, 1 - core], cs.at[t, 1, k], cr.at[t, 1, k], c_id
             )
             if first and k == 0:
+                for d in range(1, devices):
+                    source = (me + devices - d) % devices
+                    arrived(spread_in.at[source], ss.at[d], sr.at[d], {"expert": source})
+                height = own.shape[0]
+                turned = jnp.concatenate([spread_in[b] for b in range(devices)], axis=0).T
+                for b in range(devices):
+                    for at in range(TICKS):
+                        scale_ref[at, b * height : (b + 1) * height, :] = turned[
+                            at * height : (at + 1) * height, b : b + 1
+                        ]
                 for load in loads:
                     load.wait()
             group = gathered.at[t, zpeer[k]]
@@ -162,7 +206,7 @@
                 chip_sum[t, k, across].astype(jnp.float32) + x_in[t, k].astype(jnp.float32)
             ).astype(jnp.bfloat16)
             if k:
-                send(pair_sum.at[t, k], z_in.at[t, k], ts.at[t, k], tr.at[t, k], z_ids[k])
+                send(pair_sum.at[t, k], z_in.at[t, lane[k]], ts.at[t, k], tr.at[t, lane[k]], z_ids[k])
 
         for step in range(NZ + 4):
             for lag, stage in ((0, stage_a), (1, stage_b), (3, stage_d), (4, stage_e), (2, stage_c)):
@@ -199,8 +243,13 @@
     for copy in sends:
         copy.wait_send()
 
-
-def layers_call(held, entering, gain, scales, gate_w, up_w, down_w):
+    @pl.when(inner == 1)
+    def _():
+        for args in inner_sends:
+            describe(*args).wait_send()
+
+
+def layers_call(held, entering, gain, spread, gate_w, up_w, down_w):
     rows, width = held.shape
     inner = gate_w.shape[1]
     bf16 = jnp.bfloat16
@@ -226,8 +275,11 @@
             pltpu.VMEM(gate_w.shape, bf16),
             pltpu.VMEM(up_w.shape, bf16),
             pltpu.VMEM(down_w.shape, bf16),
+            pltpu.VMEM((4 * NZ, 1, TICKS * rows), jnp.float32),
+            pltpu.VMEM((TICKS, 4 * NZ * rows, 1), jnp.float32),
             dma((3,)),
-            dma((TICKS, NZ)), dma((TICKS, NZ)),
+            dma((4 * NZ,)), dma((4 * NZ,)),
+            dma((TICKS, NZ + 1)), dma((TICKS, NZ)),
             dma((TICKS, NZ)), dma((TICKS, NZ)),
             dma((TICKS, 2, NZ)), dma((TICKS, 2, NZ)),
             dma((TICKS, NZ)), dma((TICKS, NZ)),
@@ -243,18 +295,19 @@
             bytes_accessed=6 * width * inner + 8 * rows * width,
             transcendentals=tall * inner,
         ),
-    )(held, entering, gain, scales, gate_w, up_w, down_w)
+    )(held, entering, gain, spread, gate_w, up_w, down_w)
 
 
 def local(in_flight, entering, norm_gain, w_gate, w_up, w_down, routes, combine_weight):
     section_index = lax.axis_index("section")
     experts = lax.axis_size("expert") * w_gate.shape[1]
     spread = expert_weights(routes[0], combine_weight[0], experts)
-    mine = lax.all_to_all(spread, "expert", split_axis=2, concat_axis=1, tiled=True)
     if experts == 4 * NZ and lax.axis_size("section") == 2:
         return layers_call(
-            in_flight[0], entering[0], norm_gain, mine, w_gate[0, 0], w_up[0, 0], w_down[0, 0]
+            in_flight[0], entering[0], norm_gain, spread.reshape(-1, experts).T[:, None],
+            w_gate[0, 0], w_up[0, 0], w_down[0, 0],
         )[:, None]
+    mine = lax.all_to_all(spread, "expert", split_axis=2, concat_axis=1, tiled=True)
     carried = in_flight[0]
     traced = []
     for tick_index in range(TICKS):

time: 179 us -> 159 us (0.89)
  the two profiles are of different devices: /device:TPU:15 before, /device:TPU:5 now
where the time goes in v3:
time: 159 us
  Pallas kernels  156 us (98%)
  local copies, waits for them, and re-layouts  2.57 us (2%)
    pallas_call x1, Pallas kernels, layers_call(): pl.pallas_call(layers_kernel, out_shape=jax.ShapeDtypeStruct((TICKS, rows...  156 us

profile of v3, /device:TPU:5, one launch (start us, length us, event | category | flops | bytes accessed | tf_op | source)
XLA Modules:
  0.0 158.9 jit_solution(17273038524554175121)
XLA Ops:
  0.0 0.7 select_reduce_fusion
  0.8 0.7 reshape.5
  1.4 155.6 %shard_map.82 = bf16[2,64,2048]{2,1,0:T(8,128)(2,1)} custom-call(bf16[64,2048]{1,0:T(8,128)(2,1)} %bitcast.22, bf16[64,2048]{1,0:T(8,128)(2,1)} %bitcast.23, bf16[1,2048]{1,0:T(2,128)(2,1)} %gain_ref.1, f32[16,1,128]{2,1,0:T(1,128)} %bitcast.16, bf16[2048,768]{1,0:T(8,128)(2,1)} %bitcast.19, bf16[2048,768]{1,0:T(8,128)(2,1)} %bitcast.20, ...), custom_call_target="tpu_custom_call" | custom-call | flops 19327352832 | bytes 10485760 | tf_op jit(solution)/shard_map/pallas_call | solution.py:260
  157.0 1.9 %copy.15 = bf16[2,1,64,2048]{3,2,1,0:T(8,128)(2,1)} copy(bf16[2,1,64,2048]{3,2,1,0:T(8,128)(2,1)} %bitcast.15) | data formatting | bytes 1048576
  (1 shorter events, 0.0 us)

commit v4 on v3

--- a/solution.py
+++ b/solution.py
@@ -208,8 +208,8 @@
             if k:
                 send(pair_sum.at[t, k], z_in.at[t, lane[k]], ts.at[t, k], tr.at[t, lane[k]], z_ids[k])
 
-        for step in range(NZ + 4):
-            for lag, stage in ((0, stage_a), (1, stage_b), (3, stage_d), (4, stage_e), (2, stage_c)):
+        for step in range(NZ + 3):
+            for lag, stage in ((0, stage_a), (1, stage_b), (2, stage_d), (3, stage_e), (1, stage_c)):
                 if 0 <= step - lag < NZ:
                     stage(step - lag)
 

time: 159 us -> 157 us (0.987)
  the two profiles are of different devices: /device:TPU:5 before, /device:TPU:15 now
where the time goes in v4:
time: 157 us; the launch traced here: 156 us
  Pallas kernels  152 us (97%)
  local copies, waits for them, and re-layouts  2.57 us (2%)
    pallas_call x1, Pallas kernels, layers_call(): pl.pallas_call(layers_kernel, out_shape=jax.ShapeDtypeStruct((TICKS, rows...  152 us

profile of v4, /device:TPU:15, one launch (start us, length us, event | category | flops | bytes accessed | tf_op | source)
XLA Modules:
  0.0 155.5 jit_solution(4546821753630885585)
XLA Ops:
  0.0 0.7 select_reduce_fusion
  0.8 0.7 reshape.5
  1.4 152.2 %shard_map.82 = bf16[2,64,2048]{2,1,0:T(8,128)(2,1)} custom-call(bf16[64,2048]{1,0:T(8,128)(2,1)} %bitcast.22, bf16[64,2048]{1,0:T(8,128)(2,1)} %bitcast.23, bf16[1,2048]{1,0:T(2,128)(2,1)} %gain_ref.1, f32[16,1,128]{2,1,0:T(1,128)} %bitcast.16, bf16[2048,768]{1,0:T(8,128)(2,1)} %bitcast.19, bf16[2048,768]{1,0:T(8,128)(2,1)} %bitcast.20, ...), custom_call_target="tpu_custom_call" | custom-call | flops 19327352832 | bytes 10485760 | tf_op jit(solution)/shard_map/pallas_call | solution.py:260
  153.6 1.9 %copy.15 = bf16[2,1,64,2048]{3,2,1,0:T(8,128)(2,1)} copy(bf16[2,1,64,2048]{3,2,1,0:T(8,128)(2,1)} %bitcast.15) | data formatting | bytes 1048576
  (1 shorter events, 0.0 us)

commit v5 on v3

--- a/solution.py
+++ b/solution.py
@@ -151,7 +151,7 @@
             arrived(
                 gathered.at[t, zpeer[k], 1 - across, 1 - core], cs.at[t, 1, k], cr.at[t, 1, k], c_id
             )
-            if first and k == 0:
+            if first and k == 1:
                 for d in range(1, devices):
                     source = (me + devices - d) % devices
                     arrived(spread_in.at[source], ss.at[d], sr.at[d], {"expert": source})
@@ -211,7 +211,7 @@
         for step in range(NZ + 4):
             for lag, stage in ((0, stage_a), (1, stage_b), (3, stage_d), (4, stage_e), (2, stage_c)):
                 if 0 <= step - lag < NZ:
-                    stage(step - lag)
+                    stage(step - lag if lag < 2 else (step - lag + 1) % NZ)
 
         total = as_float + pair_sum[t, 0].astype(jnp.float32)
         for k in range(1, NZ):

time: 159 us -> 152 us (0.956)
  Pallas kernels: 156 us -> 148 us
    pallas_call x1, Pallas kernels: 156 us -> 148 us  [layers_call(): pl.pallas_call(layers_kernel, out_shape=jax.ShapeDtypeStruct((TICKS, rows...]
where the time goes in v5:
time: 152 us; the launch traced here: 151 us
  Pallas kernels  148 us (97%)
  local copies, waits for them, and re-layouts  2.57 us (2%)
    pallas_call x1, Pallas kernels, layers_call(): pl.pallas_call(layers_kernel, out_shape=jax.ShapeDtypeStruct((TICKS, rows...  148 us

profile of v5, /device:TPU:5, one launch (start us, length us, event | category | flops | bytes accessed | tf_op | source)
XLA Modules:
  0.0 151.3 jit_solution(4185450310882024650)
XLA Ops:
  0.0 0.7 select_reduce_fusion
  0.8 0.7 reshape.5
  1.4 147.9 %shard_map.82 = bf16[2,64,2048]{2,1,0:T(8,128)(2,1)} custom-call(bf16[64,2048]{1,0:T(8,128)(2,1)} %bitcast.22, bf16[64,2048]{1,0:T(8,128)(2,1)} %bitcast.23, bf16[1,2048]{1,0:T(2,128)(2,1)} %gain_ref.1, f32[16,1,128]{2,1,0:T(1,128)} %bitcast.16, bf16[2048,768]{1,0:T(8,128)(2,1)} %bitcast.19, bf16[2048,768]{1,0:T(8,128)(2,1)} %bitcast.20, ...), custom_call_target="tpu_custom_call" | custom-call | flops 19327352832 | bytes 10485760 | tf_op jit(solution)/shard_map/pallas_call | solution.py:260
  149.4 1.9 %copy.15 = bf16[2,1,64,2048]{3,2,1,0:T(8,128)(2,1)} copy(bf16[2,1,64,2048]{3,2,1,0:T(8,128)(2,1)} %bitcast.15) | data formatting | bytes 1048576
  (1 shorter events, 0.0 us)
